TPU v7x, 32 devices: a whole 2x2x4 slice. The times are simulated.
32 devices in a mesh: shots: 2 (over y), bx: 4 (over z), by: 2 (over x), bz: 2 (over core).
Axes of the slice: x: 2, y: 2, z: 4, core: 2. Of those that a mesh axis runs over, the one named last changes fastest.
Arguments:
- weights: bfloat16 [16384, 2, 256], P(('shots', 'bx', 'by', 'bz')), parts along dimension 0, may hold values from -6 to 6
- interp: bfloat16 [2, 2, 256, 256], replicated, may hold values from -0.25 to 0.25
- slowness: float32 [2, 2, 256], replicated, may hold values from -0.05 to 0.05
- box_coord: int32 [2, 8192], P(None, ('bx', 'by', 'bz')), may hold values from 0 to 127
Outputs:
- result: bfloat16 [16384, 2, 256], P(('shots', 'bx', 'by', 'bz')), parts along dimension 0
There are 2 independent parts, one for each index of `shots`. A program takes and returns all parts, laid end to end along the dimension named above; an argument that names none is the same for every part. Nothing has to cross between parts.
All inputs are finite; a program needn't handle non-finite values.
Results may differ from a plain program's by a relative error of at most 0.022.
Values may be sent and summed in bfloat16 or wider, within the bound.
A program may use at most 64 MiB of HBM per device.

v0:
```python
import jax
import jax.numpy as jnp
from jax import lax
from jax.sharding import PartitionSpec as P

LOCAL = 4


def from_partner(block, axis, stride):
    count = lax.axis_size(axis)
    route = []
    for low in range(count):
        high = low | 1 << stride
        if high != low and high < count:
            route += [(low, high), (high, low)]
    return lax.ppermute(block, axis, route)


def apply_matrix(block, matrix):
    block_shape = block.shape
    product = jnp.dot(
        block.reshape(-1, block_shape[-1]), matrix, preferred_element_type=jnp.float32
    )
    return product.reshape(block_shape)


def rotate_phase(summed, cosine, sine):
    real_part = summed[..., 0, :]
    imag_part = summed[..., 1, :]
    return jnp.stack(
        [cosine * real_part - sine * imag_part, sine * real_part + cosine * imag_part], axis=-2
    ).astype(jnp.bfloat16)


def level_step(grouped, interp, cos_group, sin_group):
    first_child = grouped[:, 0]
    second_child = grouped[:, 1]
    results = []
    for target in range(2):
        summed = apply_matrix(first_child, interp[target, 0]) + apply_matrix(
            second_child, interp[target, 1]
        )
        results.append(rotate_phase(summed, cos_group[:, target], sin_group[:, target]))
    return jnp.stack(results, axis=1)


def partner_step(current, partner, upper_bit, interp, cosine, sine):
    mine_part = apply_matrix(current, interp[upper_bit, upper_bit])
    other_part = apply_matrix(partner, interp[upper_bit, 1 - upper_bit])
    return rotate_phase(mine_part + other_part, cosine, sine)


def local(weights, interp, slowness, box_coord):
    per_dev = weights.shape[0]
    rank_size = weights.shape[2]
    coords = box_coord.astype(jnp.float32)
    dist_angle = (
        coords[0][:, None] * slowness[0, 0][None, :] + coords[1][:, None] * slowness[0, 1][None, :]
    )
    local_angle = (
        coords[0][:, None] * slowness[1, 0][None, :] + coords[1][:, None] * slowness[1, 1][None, :]
    )
    dist_cos = jnp.cos(dist_angle)
    dist_sin = jnp.sin(dist_angle)
    local_cos = jnp.cos(local_angle)
    local_sin = jnp.sin(local_angle)
    current = weights
    bit_num = 0
    partner = from_partner(current, "bz", bit_num)
    upper_bit = lax.axis_index("bz") >> bit_num & 1
    current = partner_step(current, partner, upper_bit, interp, dist_cos, dist_sin)
    for bit_num in range(lax.axis_size("by").bit_length() - 1):
        partner = from_partner(current, "by", bit_num)
        upper_bit = lax.axis_index("by") >> bit_num & 1
        current = partner_step(current, partner, upper_bit, interp, dist_cos, dist_sin)
    for bit_num in range(lax.axis_size("bx").bit_length() - 1):
        partner = from_partner(current, "bx", bit_num)
        upper_bit = lax.axis_index("bx") >> bit_num & 1
        current = partner_step(current, partner, upper_bit, interp, dist_cos, dist_sin)
    for local_num in range(LOCAL):
        span_len = per_dev >> local_num + 1
        grouped = current.reshape(-1, 2, span_len, 2, rank_size)
        cos_group = local_cos.reshape(-1, 2, span_len, rank_size)
        sin_group = local_sin.reshape(-1, 2, span_len, rank_size)
        current = level_step(grouped, interp, cos_group, sin_group).reshape(per_dev, 2, rank_size)
    return current


def solution(mesh):
    placed = (P(("shots", "bx", "by", "bz"), None, None), P(), P(), P(None, ("bx", "by", "bz")))
    return jax.shard_map(
        local,
        mesh=mesh,
        in_specs=placed,
        out_specs=P(("shots", "bx", "by", "bz"), None, None),
        check_vma=False,
    )
```

profile of v0, /device:TPU:0, one launch (start us, length us, event | category | flops | bytes accessed | tf_op | source)
XLA Modules:
  0.0 79.9 jit_solution(11181130146163404498)
XLA Ops:
  0.0 0.5 collective-permute-start
  0.5 0.8 fusion.121
  1.2 1.3 %reshape.1078 = bf16[1024,256]{1,0:T(8,128)(2,1)S(1)} reshape(bf16[512,2,256]{2,1,0:T(2,128)(2,1)} %param.4) | data formatting | bytes 1048576 | tf_op jit(solution)/shard_map/reshape | solution.py:22
  2.5 0.7 copy-done.1
  3.3 0.4 fusion.80
  3.8 0.4 fusion
  4.2 1.3 %copy.43 = f32[1024,256]{1,0:T(8,128)} copy(f32[1024,256]{0,1:T(8,128)S(1)} %fusion) | data formatting | bytes 2097152 | tf_op jit(solution)/shard_map/add | solution.py:50
  5.5 1.8 %add.191 = f32[512,2,256]{2,1,0:T(2,128)S(1)} reshape(f32[1024,256]{1,0:T(8,128)} %copy.43) | data formatting | bytes 2097152 | tf_op jit(solution)/shard_map/add | solution.py:50
  7.4 0.8 %fusion.120 = (f32[512,1,256]{2,1,0:T(1,128)S(1)}, f32[512,1,256]{2,1,0:T(1,128)S(1)}) fusion(f32[512,2,256]{2,1,0:T(2,128)S(1)} %add.191), kind=kLoop, calls=%fused_computation.194 | loop fusion | bytes 2097152 | tf_op jit(solution)/shard_map/slice | solution.py:28
  8.2 2.6 %subtract_convert_fusion.3 = (bf16[512,1,256]{2,0,1:T(8,128)(2,1)S(1)}, bf16[512,1,256]{2,0,1:T(8,128)(2,1)S(1)}) fusion(f32[512,1,256]{2,1,0:T(1,128)S(1)} %get-tuple-element.31, f32[512,1,256]{2,1,0:T(1,128)S(1)} %get-tuple-element.30, f32[256]{0:T(256)S(1)} %bitcast.454, f32[512]{0:T(512)S(1)} %bitcast.436, f32[256]{0:T(256)S(1)} %bitcast.450, ...), kind=kLoop, calls=%fused_computation.31 | loop fusion | flops 1441792 | bytes 1579008 | tf_op jit(solution)/shard_map/convert.40
  10.8 2.6 %collective-permute-start.1 = (bf16[512,2,256]{2,0,1:T(8,128)(2,1)S(1)}, bf16[512,2,256]{2,0,1:T(8,128)(2,1)S(1)}, u32[]{:S(2)}, u32[]{:S(2)}) collective-permute-start(bf16[512,2,256]{2,0,1:T(8,128)(2,1)S(1)} %pad_maximum_fusion), channel_id=1, source_target_pairs={{0,2},{2,0},{1,3},{3,1},{4,6},{6,4},{5,7},{7,5},{8,10},{10,8},{9,1... | collective-permute-start | bytes 1572872 | tf_op jit(solution)/shard_map/ppermute | solution.py:16
  14.1 11.9 %collective-permute-done.1 = bf16[512,2,256]{2,0,1:T(8,128)(2,1)S(1)} collective-permute-done((bf16[512,2,256]{2,0,1:T(8,128)(2,1)S(1)}, bf16[512,2,256]{2,0,1:T(8,128)(2,1)S(1)}, u32[]{:S(2)}, u32[]{:S(2)}) %collective-permute-start.1) | collective-permute-done | bytes 524320 | tf_op jit(solution)/shard_map/ppermute | solution.py:16
  26.3 2.4 %subtract_convert_fusion.2 = (bf16[512,1,256]{2,0,1:T(8,128)(2,1)S(1)}, bf16[512,1,256]{2,0,1:T(8,128)(2,1)S(1)}) fusion(f32[512,2,256]{2,0,1:T(8,128)S(1)} %convolution_add_fusion.2, f32[256]{0:T(256)S(1)} %bitcast.455, f32[512]{0:T(512)S(1)} %bitcast.440, f32[256]{0:T(256)S(1)} %bitcast.451, f32[512]{0:T(512)S(1)} %bitcast.447), kind=kLoop, calls=%fused_computation.29 | loop fusion | flops 1441792 | bytes 1579008 | tf_op jit(solution)/shard_map/convert.38
  28.7 1.9 %collective-permute-start.2 = (bf16[512,2,256]{2,0,1:T(8,128)(2,1)S(1)}, bf16[512,2,256]{2,0,1:T(8,128)(2,1)S(1)}, u32[]{:S(2)}, u32[]{:S(2)}) collective-permute-start(bf16[512,2,256]{2,0,1:T(8,128)(2,1)S(1)} %pad_maximum_fusion.1), channel_id=1, source_target_pairs={{0,4},{4,0},{8,12},{12,8},{1,5},{5,1},{9,13},{13,9},{2,6},{6,2},{1... | collective-permute-start | bytes 1572872 | tf_op jit(solution)/shard_map/ppermute | solution.py:16
  30.6 2.0 %fusion.5 = (f32[1,2,256,256]{3,2,1,0:T(8,128)S(1)}, f32[1,2,256,256]{3,2,1,0:T(8,128)S(1)}) fusion(f32[256]{0:T(256)S(1)} %bitcast.458, f32[2,256]{1,0:T(2,128)S(1)} %mul.422, f32[256]{0:T(256)S(1)} %bitcast.462, f32[2,256]{1,0:T(2,128)S(1)} %mul.418), kind=kLoop, calls=%fused_computation.36 | loop fusion | flops 393216 | bytes 1054720 | tf_op jit(solution)/shard_map/sin | solution.py:66
  32.6 2.0 %fusion.9 = (f32[4,2,64,256]{3,2,0,1:T(8,128)S(1)}, f32[4,2,64,256]{3,2,0,1:T(8,128)S(1)}) fusion(f32[256]{0:T(256)S(1)} %bitcast.459, f32[4,2,64]{2,0,1:T(4,128)S(1)} %copy.40, f32[256]{0:T(256)S(1)} %bitcast.463, f32[4,2,64]{2,0,1:T(4,128)S(1)} %copy.39), kind=kLoop, calls=%fused_computation.42 | loop fusion | flops 393216 | bytes 1054720 | tf_op jit(solution)/shard_map/sin | solution.py:66
  35.0 7.6 %collective-permute-done.2 = bf16[512,2,256]{2,0,1:T(8,128)(2,1)S(1)} collective-permute-done((bf16[512,2,256]{2,0,1:T(8,128)(2,1)S(1)}, bf16[512,2,256]{2,0,1:T(8,128)(2,1)S(1)}, u32[]{:S(2)}, u32[]{:S(2)}) %collective-permute-start.2) | collective-permute-done | bytes 524320 | tf_op jit(solution)/shard_map/ppermute | solution.py:16
  42.8 2.4 %subtract_convert_fusion.1 = (bf16[512,1,256]{2,0,1:T(8,128)(2,1)S(1)}, bf16[512,1,256]{2,0,1:T(8,128)(2,1)S(1)}) fusion(f32[512,2,256]{2,0,1:T(8,128)S(1)} %convolution_add_fusion.1, f32[256]{0:T(256)S(1)} %bitcast.456, f32[512]{0:T(512)S(1)} %bitcast.441, f32[256]{0:T(256)S(1)} %bitcast.452, f32[512]{0:T(512)S(1)} %bitcast.448), kind=kLoop, calls=%fused_computation.27 | loop fusion | flops 1441792 | bytes 1579008 | tf_op jit(solution)/shard_map/convert.36
  45.3 2.7 %collective-permute-start.3 = (bf16[512,2,256]{2,0,1:T(8,128)(2,1)S(1)}, bf16[512,2,256]{2,0,1:T(8,128)(2,1)S(1)}, u32[]{:S(2)}, u32[]{:S(2)}) collective-permute-start(bf16[512,2,256]{2,0,1:T(8,128)(2,1)S(1)} %pad_maximum_fusion.2), channel_id=1, source_target_pairs={{0,8},{8,0},{4,12},{12,4},{1,9},{9,1},{5,13},{13,5},{2,10},{10,2},... | collective-permute-start | bytes 1572872 | tf_op jit(solution)/shard_map/ppermute | solution.py:16
  48.0 2.0 %fusion.7 = (f32[2,2,128,256]{3,2,0,1:T(8,128)S(1)}, f32[2,2,128,256]{3,2,0,1:T(8,128)S(1)}) fusion(f32[256]{0:T(256)S(1)} %bitcast.460, f32[2,2,128]{2,0,1:T(2,128)S(1)} %copy.42, f32[256]{0:T(256)S(1)} %bitcast.464, f32[2,2,128]{2,0,1:T(2,128)S(1)} %copy.41), kind=kLoop, calls=%fused_computation.39 | loop fusion | flops 393216 | bytes 1054720 | tf_op jit(solution)/shard_map/sin | solution.py:66
  50.0 2.0 %fusion.11 = (f32[8,2,32,256]{3,2,0,1:T(8,128)S(1)}, f32[8,2,32,256]{3,2,0,1:T(8,128)S(1)}) fusion(f32[256]{0:T(256)S(1)} %bitcast.461, f32[8,2,32]{2,0,1:T(8,128)S(1)} %copy.38, f32[256]{0:T(256)S(1)} %bitcast.465, f32[8,2,32]{2,0,1:T(8,128)S(1)} %copy.37), kind=kLoop, calls=%fused_computation.45 | loop fusion | flops 393216 | bytes 1054720 | tf_op jit(solution)/shard_map/sin | solution.py:66
  52.4 18.0 %collective-permute-done.3 = bf16[512,2,256]{2,0,1:T(8,128)(2,1)S(1)} collective-permute-done((bf16[512,2,256]{2,0,1:T(8,128)(2,1)S(1)}, bf16[512,2,256]{2,0,1:T(8,128)(2,1)S(1)}, u32[]{:S(2)}, u32[]{:S(2)}) %collective-permute-start.3) | collective-permute-done | bytes 524320 | tf_op jit(solution)/shard_map/ppermute | solution.py:16
  70.7 2.6 %add_convert_fusion = (bf16[512,1,256]{2,0,1:T(8,128)(2,1)S(1)}, bf16[512,1,256]{2,0,1:T(8,128)(2,1)S(1)}) fusion(f32[512,2,256]{2,0,1:T(8,128)S(1)} %convolution_add_fusion, f32[256]{0:T(256)S(1)} %bitcast.457, f32[512]{0:T(512)S(1)} %bitcast.442, f32[256]{0:T(256)S(1)} %bitcast.453, f32[512]{0:T(512)S(1)} %bitcast.449), kind=kLoop, calls=%fused_computation.24 | loop fusion | flops 1441792 | bytes 1579008 | tf_op jit(solution)/shard_map/convert.34
  78.6 1.3 %copy.77 = bf16[512,2,256]{2,1,0:T(2,128)(2,1)} copy(bf16[512,2,256]{2,0,1:T(8,128)(2,1)S(1)} %bitcast.431) | data formatting | bytes 1048576 | tf_op jit(solution)/shard_map/reshape | solution.py:85
  (61 shorter events, 7.6 us)
Async XLA Ops:
  0.0 3.6 %collective-permute-start = (bf16[512,2,256]{2,1,0:T(2,128)(2,1)}, bf16[512,2,256]{2,1,0:T(2,128)(2,1)S(1)}, u32[]{:S(2)}, u32[]{:S(2)}) collective-permute-start(bf16[512,2,256]{2,1,0:T(2,128)(2,1)} %param.4), channel_id=1, source_target_pairs={{0,1},{1,0},{2,3},{3,2},{4,5},{5,4},{6,7},{7,6},{8,9},{9,8},{10,11... | collective-permute-start | bytes 1572872 | tf_op jit(solution)/shard_map/ppermute | solution.py:16
  1.2 2.0 %copy-start = (bf16[2,2,256,256]{3,2,1,0:T(8,128)(2,1)S(1)}, bf16[2,2,256,256]{3,2,1,0:T(8,128)(2,1)}, u32[]{:S(2)}) copy-start(bf16[2,2,256,256]{3,2,1,0:T(8,128)(2,1)} %param.5) | copy-start | bytes 1572868
  2.5 0.7 copy-start.1
  10.8 15.1 %collective-permute-start.1 = (bf16[512,2,256]{2,0,1:T(8,128)(2,1)S(1)}, bf16[512,2,256]{2,0,1:T(8,128)(2,1)S(1)}, u32[]{:S(2)}, u32[]{:S(2)}) collective-permute-start(bf16[512,2,256]{2,0,1:T(8,128)(2,1)S(1)} %pad_maximum_fusion), channel_id=1, source_target_pairs={{0,2},{2,0},{1,3},{3,1},{4,6},{6,4},{5,7},{7,5},{8,10},{10,8},{9,1... | collective-permute-start | bytes 1572872 | tf_op jit(solution)/shard_map/ppermute | solution.py:16
  28.7 13.8 %collective-permute-start.2 = (bf16[512,2,256]{2,0,1:T(8,128)(2,1)S(1)}, bf16[512,2,256]{2,0,1:T(8,128)(2,1)S(1)}, u32[]{:S(2)}, u32[]{:S(2)}) collective-permute-start(bf16[512,2,256]{2,0,1:T(8,128)(2,1)S(1)} %pad_maximum_fusion.1), channel_id=1, source_target_pairs={{0,4},{4,0},{8,12},{12,8},{1,5},{5,1},{9,13},{13,9},{2,6},{6,2},{1... | collective-permute-start | bytes 1572872 | tf_op jit(solution)/shard_map/ppermute | solution.py:16
  45.3 25.1 %collective-permute-start.3 = (bf16[512,2,256]{2,0,1:T(8,128)(2,1)S(1)}, bf16[512,2,256]{2,0,1:T(8,128)(2,1)S(1)}, u32[]{:S(2)}, u32[]{:S(2)}) collective-permute-start(bf16[512,2,256]{2,0,1:T(8,128)(2,1)S(1)} %pad_maximum_fusion.2), channel_id=1, source_target_pairs={{0,8},{8,0},{4,12},{12,4},{1,9},{9,1},{5,13},{13,5},{2,10},{10,2},... | collective-permute-start | bytes 1572872 | tf_op jit(solution)/shard_map/ppermute | solution.py:16
where the time goes:
time: 80.1 us; the launch traced here: 79.9 us
  waiting for transfers between devices  37.5 us (47%)
  other arithmetic  19.4 us (24%)
  local copies, waits for them, and re-layouts  8.88 us (11%)
  starting transfers between devices  7.61 us (10%)
  matrix products  6.14 us (8%)
    ppermute x4, waiting for transfers between devices, from_partner(): return lax.ppermute(block, axis, route)  37.5 us
    another operation x5, other arithmetic  10.1 us
    sin x4, other arithmetic, local(): local_sin = jnp.sin(local_angle)  8.09 us
    ppermute x4, starting transfers between devices, from_partner(): return lax.ppermute(block, axis, route)  7.61 us
    dot_general x24, matrix products, apply_matrix(): jnp.dot(block.reshape(-1, block_shape[-1]), matrix, preferred_element_typ...  6.14 us
    add x2, local copies, waits for them, and re-layouts, partner_step(): return rotate_phase(mine_part + other_part, cosine, sine)  3.16 us
  transfers between devices with their start and end apart: 4, of which 3 were waited for; matrix products, arithmetic and copies ran while one was open for 15% of the time, Pallas kernels for 0%

commit v1 on v0

v1 whole, which is shorter than its diff:
```python
import functools
import math

import jax
import jax.numpy as jnp
from jax import lax
from jax.experimental import pallas as pl
from jax.experimental.pallas import tpu as pltpu
from jax.sharding import PartitionSpec as P

LOCAL = 4
MESH = pl.DeviceIdType.MESH
F32 = jnp.float32
BF16 = jnp.bfloat16
SUB = 8

SIN_TERMS = [(-1) ** i * math.pi ** (2 * i + 1) / math.factorial(2 * i + 1) for i in range(6)]
COS_TERMS = [(-1) ** i * math.pi ** (2 * i) / math.factorial(2 * i) for i in range(6)]


def horner(terms, square):
    total = jnp.full_like(square, terms[-1])
    for term in terms[-2::-1]:
        total = total * square + term
    return total


def cos_sin(angle):
    turns = angle * (1.0 / (2.0 * math.pi))
    frac = turns - jnp.round(turns)
    square = frac * frac
    half_sin = frac * horner(SIN_TERMS, square)
    half_cos = horner(COS_TERMS, square)
    return 1.0 - 2.0 * half_sin * half_sin, 2.0 * half_sin * half_cos


def shuffle_matrix(rows, inverse):
    worked = lax.broadcasted_iota(jnp.int32, (rows, rows), 1 if inverse else 0)
    stored = lax.broadcasted_iota(jnp.int32, (rows, rows), 0 if inverse else 1)
    source = (
        (worked // 32) * 32
        + (worked % 8) * 4
        + ((worked // 16) % 2) * 2
        + (worked // 8) % 2
    )
    return jnp.where(stored == source, 1.0, 0.0).astype(BF16)


def rotate(summed, cosine, sine):
    real_part, imag_part = summed[:, 0], summed[:, 1]
    return jnp.stack(
        [cosine * real_part - sine * imag_part, sine * real_part + cosine * imag_part], axis=1
    )


def dot(a, b):
    return jnp.dot(a, b, preferred_element_type=F32)


def kernel(
    levels, w_ref, interp_ref, slow_ref, coord_ref, out_ref,
    cur, got, dcos, dsin, lcos, lsin, padded, columns, send_sem, recv_sem,
):
    depth = len(levels)
    high, nk = w_ref.shape[0], w_ref.shape[1]
    half = high // 2
    chunks = 2 * nk
    rows = half * 2 * SUB
    rank = interp_ref.shape[-1]

    upper, partner = [], []
    for axis, bit in levels:
        me = lax.axis_index(axis)
        up = (me // (1 << bit)) % 2
        upper.append(up)
        partner.append({axis: me + (1 << bit) * (1 - 2 * up)})

    barrier = pltpu.get_barrier_semaphore()
    for device in partner:
        pl.semaphore_signal(barrier, inc=1, device_id=device, device_id_type=MESH)
    pl.semaphore_wait(barrier, depth)

    def copy(level, m):
        return pltpu.make_async_remote_copy(
            src_ref=cur.at[level, m],
            dst_ref=got.at[level, m],
            send_sem=send_sem.at[level, m],
            recv_sem=recv_sem.at[level, m],
            device_id=partner[level],
            device_id_type=MESH,
        )

    spread = shuffle_matrix(half * 32, False)

    def load(m):
        k, top = m // 2, (m % 2) * half
        stored = w_ref[top : top + half, k].reshape(half * 32, 128)
        moved = dot(spread, stored).reshape(half, 2, 2 * SUB, 128)
        block = jnp.concatenate([moved[:, 0], moved[:, 1]], axis=-1)
        cur[0, m] = block.reshape(rows, rank).astype(BF16)
        copy(0, m).start()

    def angles(m, table, cos_ref, sin_ref):
        k, top = m // 2, (m % 2) * half
        column = columns[top : top + half, k].reshape(half * SUB, 8)
        angle = column[:, 0:1] * slow_ref[table, 0:1] + column[:, 1:2] * slow_ref[table, 1:2]
        cosine, sine = cos_sin(angle)
        cos_ref[m] = cosine.reshape(half, SUB, rank)
        sin_ref[m] = sine.reshape(half, SUB, rank)

    def device_step(level, m):
        up = upper[level]
        mine = dot(cur[level, m], interp_ref[up, up])
        copy(level, m).wait_recv()
        summed = mine + dot(got[level, m], interp_ref[up, 1 - up])
        turned = rotate(summed.reshape(half, 2, SUB, rank), dcos[m], dsin[m])
        cur[level + 1, m] = turned.reshape(rows, rank).astype(BF16)
        if level + 1 < depth:
            copy(level + 1, m).start()

    gather = shuffle_matrix(half * 32, True)

    def local_steps(k):
        block = cur[depth, 2 * k : 2 * k + 2].reshape(high, 2 * SUB, rank)
        cosine = lcos[2 * k : 2 * k + 2].reshape(high, SUB, rank)
        sine = lsin[2 * k : 2 * k + 2].reshape(high, SUB, rank)
        for num in range(LOCAL):
            outer, inner = 1 << num, high >> (num + 1)
            pair = block.reshape(outer, 2, inner, 2 * SUB, rank)
            first = pair[:, 0].reshape(-1, rank)
            second = pair[:, 1].reshape(-1, rank)
            cos_pair = cosine.reshape(outer, 2, inner, SUB, rank)
            sin_pair = sine.reshape(outer, 2, inner, SUB, rank)
            results = []
            for target in range(2):
                summed = dot(first, interp_ref[target, 0]) + dot(second, interp_ref[target, 1])
                turned = rotate(
                    summed.reshape(outer * inner, 2, SUB, rank),
                    cos_pair[:, target].reshape(-1, SUB, rank),
                    sin_pair[:, target].reshape(-1, SUB, rank),
                )
                results.append(turned.astype(BF16).reshape(outer, inner, 2 * SUB, rank))
            block = jnp.stack(results, axis=1).reshape(high, 2 * SUB, rank)
        for part in range(2):
            top = part * half
            piece = block[top : top + half]
            worked = jnp.stack([piece[..., :128], piece[..., 128:]], axis=1)
            stored = dot(gather, worked.reshape(half * 32, 128))
            out_ref[top : top + half, k] = stored.reshape(half, 32, 128).astype(BF16)

    for m in range(chunks):
        load(m)
    padded[...] = jnp.zeros_like(padded)
    padded[0:2] = coord_ref[...].astype(F32)
    columns[...] = padded[...].T.reshape(columns.shape)

    tasks = []
    for level in range(depth):
        rate = 0.2 if level == 0 else 2.6 if level == depth - 1 else 1.4
        for m in range(chunks):
            tasks.append((2.5 * level + rate * m, 1, "device", level, m))
    for m in range(chunks):
        tasks.append((0.2 * m, 0, "dist", 0, m))
        tasks.append((3.0 + 1.2 * m, 2, "local", 0, m))
    for k in range(nk):
        tasks.append((2.5 * (depth - 1) + 2.6 * (2 * k + 1), 3, "steps", 0, k))
    for _, _, kind, level, m in sorted(tasks):
        if kind == "device":
            device_step(level, m)
        elif kind == "dist":
            angles(m, 0, dcos, dsin)
        elif kind == "local":
            angles(m, 1, lcos, lsin)
        else:
            local_steps(m)

    for level in range(depth):
        for m in range(chunks):
            copy(level, m).wait_send()


def solution(mesh):
    levels = []
    for axis in ("bz", "by", "bx"):
        levels += [(axis, bit) for bit in range(mesh.shape[axis].bit_length() - 1)]

    def local(weights, interp, slowness, box_coord):
        per_dev, _, rank = weights.shape
        high = 1 << LOCAL
        nk = per_dev // (high * SUB)
        half = high // 2
        depth, chunks, rows = len(levels), 2 * nk, half * 2 * SUB
        stored = weights.reshape(per_dev, 2, 2, 128).transpose(0, 2, 1, 3)
        stored = stored.reshape(high, nk, 4 * SUB, 128)
        table = pltpu.VMEM((chunks, half, SUB, rank), F32)
        result = pl.pallas_call(
            functools.partial(kernel, levels),
            out_shape=jax.ShapeDtypeStruct(stored.shape, BF16),
            in_specs=[pl.BlockSpec(memory_space=pltpu.VMEM)] * 4,
            out_specs=pl.BlockSpec(memory_space=pltpu.VMEM),
            scratch_shapes=[
                pltpu.VMEM((depth + 1, chunks, rows, rank), BF16),
                pltpu.VMEM((depth, chunks, rows, rank), BF16),
                table, table, table, table,
                pltpu.VMEM((8, per_dev), F32),
                pltpu.VMEM((high, nk, SUB, 8), F32),
                pltpu.SemaphoreType.DMA((depth, chunks)),
                pltpu.SemaphoreType.DMA((depth, chunks)),
            ],
            compiler_params=pltpu.CompilerParams(
                collective_id=0, has_side_effects=True, vmem_limit_bytes=48 * 1024 * 1024
            ),
        )(stored, interp, slowness, box_coord)
        result = result.reshape(per_dev, 2, 2, 128).transpose(0, 2, 1, 3)
        return result.reshape(per_dev, 2, rank)

    return jax.shard_map(
        local,
        mesh=mesh,
        in_specs=(P(("shots", "bx", "by", "bz"), None, None), P(), P(), P(None, ("bx", "by", "bz"))),
        out_specs=P(("shots", "bx", "by", "bz"), None, None),
        check_vma=False,
    )
```

time: 80.1 us -> 44.1 us (0.55)
  Pallas kernels: 0 us -> 39.5 us
  waiting for transfers between devices: 37.5 us -> 0 us
  other arithmetic: 19.4 us -> 0 us
  starting transfers between devices: 7.61 us -> 0 us
  matrix products: 6.14 us -> 0 us
  local copies, waits for them, and re-layouts: 8.88 us -> 4.25 us
    pallas_call x0 -> x1, Pallas kernels: none -> 39.5 us  [local(): pl.pallas_call(functools.partial(kernel, levels), out_shape=jax.ShapeDtyp...]
    ppermute x4 -> x0, waiting for transfers between devices: 37.5 us -> none  [from_partner(): return lax.ppermute(block, axis, route)]
    another operation x18 -> x0, other arithmetic: 11.3 us -> none
    sin x4 -> x0, other arithmetic: 8.09 us -> none  [local(): local_sin = jnp.sin(local_angle)]
    ppermute x4 -> x0, starting transfers between devices: 7.61 us -> none  [from_partner(): return lax.ppermute(block, axis, route)]
    dot_general x24 -> x0, matrix products: 6.14 us -> none  [apply_matrix(): jnp.dot(block.reshape(-1, block_shape[-1]), matrix, preferred_element_typ...]
    unnamed x4 -> x9, local copies, waits for them, and re-layouts: 0.69 us -> 4.25 us
    add x2 -> x0, local copies, waits for them, and re-layouts: 3.16 us -> none  [partner_step(): return rotate_phase(mine_part + other_part, cosine, sine)]
  transfers between devices with their start and end apart: 4 -> 0, of which waited for: 3 -> 0; matrix products, arithmetic and copies ran while one was open for 15% -> 0% of each run, Pallas kernels for 0% -> 0%
where the time goes in v1:
time: 44.1 us; the launch traced here: 43.8 us
  Pallas kernels  39.5 us (90%)
  local copies, waits for them, and re-layouts  4.25 us (10%)
    pallas_call x1, Pallas kernels, local(): pl.pallas_call(functools.partial(kernel, levels), out_shape=jax.ShapeDtyp...  39.5 us
    unnamed x9, local copies, waits for them, and re-layouts  4.25 us

profile of v1, /device:TPU:0, one launch (start us, length us, event | category | flops | bytes accessed | tf_op | source)
XLA Modules:
  0.0 43.8 jit_solution(16338565162941616353)
XLA Ops:
  0.0 0.0 copy-start
  0.0 1.0 %copy-done = bf16[512,2,256]{2,1,0:T(2,128)(2,1)S(1)} copy-done((bf16[512,2,256]{2,1,0:T(2,128)(2,1)S(1)}, bf16[512,2,256]{2,1,0:T(2,128)(2,1)}, u32[]{:S(2)}) %copy-start) | copy-done | bytes 524312
  1.0 0.0 copy-start.1
  1.0 1.0 %copy-done.1 = bf16[2,2,256,256]{3,2,1,0:T(8,128)(2,1)S(1)} copy-done((bf16[2,2,256,256]{3,2,1,0:T(8,128)(2,1)S(1)}, bf16[2,2,256,256]{3,2,1,0:T(8,128)(2,1)}, u32[]{:S(2)}) %copy-start.1) | copy-done | bytes 524312
  2.1 0.0 copy-start.2
  2.1 0.7 %copy-done.2 = f32[2,2,256]{2,1,0:T(2,128)S(1)} copy-done((f32[2,2,256]{2,1,0:T(2,128)S(1)}, f32[2,2,256]{2,1,0:T(2,128)}, u32[]{:S(2)}) %copy-start.2) | copy-done | bytes 4120
  2.8 0.0 copy-start.3
  2.8 0.7 %copy-done.3 = s32[2,512]{1,0:T(2,128)S(1)} copy-done((s32[2,512]{1,0:T(2,128)S(1)}, s32[2,512]{1,0:T(2,128)}, u32[]{:S(2)}) %copy-start.3) | copy-done | bytes 4120
  3.5 39.5 %shard_map.46 = bf16[16,4,32,128]{3,2,1,0:T(8,128)(2,1)S(1)} custom-call(bf16[16,4,32,128]{3,2,1,0:T(8,128)(2,1)S(1)} %bitcast.11, bf16[2,2,256,256]{3,2,1,0:T(8,128)(2,1)S(1)} %copy-done.1, f32[2,2,256]{2,1,0:T(2,128)S(1)} %copy-done.2, s32[2,512]{1,0:T(2,128)S(1)} %copy-done.3), custom_call_target="tpu_custom_call" | custom-call | tf_op jit(solution)/shard_map/pallas_call | solution.py:196
  43.0 0.8 %copy.8 = bf16[512,2,256]{2,1,0:T(2,128)(2,1)} copy(bf16[512,2,256]{2,1,0:T(2,128)(2,1)S(1)} %bitcast.10) | data formatting | bytes 1048576
Async XLA Ops:
  0.0 1.0 %copy-start = (bf16[512,2,256]{2,1,0:T(2,128)(2,1)S(1)}, bf16[512,2,256]{2,1,0:T(2,128)(2,1)}, u32[]{:S(2)}) copy-start(bf16[512,2,256]{2,1,0:T(2,128)(2,1)} %param.4) | copy-start | bytes 1572868
  1.0 1.0 %copy-start.1 = (bf16[2,2,256,256]{3,2,1,0:T(8,128)(2,1)S(1)}, bf16[2,2,256,256]{3,2,1,0:T(8,128)(2,1)}, u32[]{:S(2)}) copy-start(bf16[2,2,256,256]{3,2,1,0:T(8,128)(2,1)} %interp_ref.1) | copy-start | bytes 1572868
  2.1 0.7 %copy-start.2 = (f32[2,2,256]{2,1,0:T(2,128)S(1)}, f32[2,2,256]{2,1,0:T(2,128)}, u32[]{:S(2)}) copy-start(f32[2,2,256]{2,1,0:T(2,128)} %slow_ref.1) | copy-start | bytes 12292
  2.8 0.7 %copy-start.3 = (s32[2,512]{1,0:T(2,128)S(1)}, s32[2,512]{1,0:T(2,128)}, u32[]{:S(2)}) copy-start(s32[2,512]{1,0:T(2,128)} %coord_ref.1) | copy-start | bytes 12292

commit v2 on v1

v2 whole, which is shorter than its diff:
```python
import functools
import math

import jax
import jax.numpy as jnp
from jax import lax
from jax.experimental import pallas as pl
from jax.experimental.pallas import tpu as pltpu
from jax.sharding import PartitionSpec as P

LOCAL = 4
MESH = pl.DeviceIdType.MESH
F32 = jnp.float32
BF16 = jnp.bfloat16
SUB = 8

SIN_TERMS = [(-1) ** i * math.pi ** (2 * i + 1) / math.factorial(2 * i + 1) for i in range(6)]
COS_TERMS = [(-1) ** i * math.pi ** (2 * i) / math.factorial(2 * i) for i in range(6)]


def horner(terms, square):
    total = jnp.full_like(square, terms[-1])
    for term in terms[-2::-1]:
        total = total * square + term
    return total


def cos_sin(angle):
    turns = angle * (1.0 / (2.0 * math.pi))
    frac = turns - jnp.round(turns)
    square = frac * frac
    half_sin = frac * horner(SIN_TERMS, square)
    half_cos = horner(COS_TERMS, square)
    return 1.0 - 2.0 * half_sin * half_sin, 2.0 * half_sin * half_cos


def shuffle_matrix(rows, inverse):
    worked = lax.broadcasted_iota(jnp.int32, (rows, rows), 1 if inverse else 0)
    stored = lax.broadcasted_iota(jnp.int32, (rows, rows), 0 if inverse else 1)
    source = (
        (worked // 32) * 32
        + (worked % 8) * 4
        + ((worked // 16) % 2) * 2
        + (worked // 8) % 2
    )
    return jnp.where(stored == source, 1.0, 0.0).astype(BF16)


def rotate(summed, cosine, sine):
    real_part, imag_part = summed[:, 0], summed[:, 1]
    return jnp.stack(
        [cosine * real_part - sine * imag_part, sine * real_part + cosine * imag_part], axis=1
    )


def dot(a, b):
    return jnp.dot(a, b, preferred_element_type=F32)


def kernel(
    levels, w_hbm, interp_hbm, slow_hbm, coord_hbm, out_ref,
    w_ref, interp_ref, slow_ref, coord_ref, raw, done, cur, got,
    dcos, dsin, lcos, lsin, padded, columns,
    in_sem, send_sem, recv_sem, raw_send, raw_recv, coord_send, coord_recv, done_send, done_recv,
):
    depth = len(levels)
    top = depth - 1
    high, nk = w_ref.shape[0], w_ref.shape[1]
    half = high // 2
    rows = half * 2 * SUB
    rank = interp_ref.shape[-1]
    nd, nf = nk // 2, nk // 4
    direct, owned = 2 * nd, 2 * nf
    items = direct + 2 * owned

    upper, partner = [], []
    for axis, bit in levels:
        me = lax.axis_index(axis)
        up = (me // (1 << bit)) % 2
        upper.append(up)
        partner.append({axis: me + (1 << bit) * (1 - 2 * up)})
    side = upper[top]

    def group_of(item):
        if item < direct:
            return item // 2
        return nd + side * nf + ((item - direct) % owned) // 2

    def fetch(src, dst, n):
        return pltpu.make_async_copy(src, dst, in_sem.at[n])

    fetches = [
        fetch(w_hbm.at[:, group_of(2 * n)], w_ref.at[:, group_of(2 * n)], n) for n in range(nd + nf)
    ]
    fetch_coord = fetch(coord_hbm, coord_ref.at[0], nd + nf)
    fetch_slow = fetch(slow_hbm, slow_ref, nd + nf + 1)
    fetch_interp = fetch(interp_hbm, interp_ref, nd + nf + 2)
    for one in [fetches[0], fetch_coord, fetch_slow, fetch_interp] + fetches[1:]:
        one.start()

    barrier = pltpu.get_barrier_semaphore()
    for device in partner:
        pl.semaphore_signal(barrier, inc=1, device_id=device, device_id_type=MESH)
    pl.semaphore_wait(barrier, depth)

    def remote(src, dst, sent, received, level):
        return pltpu.make_async_remote_copy(
            src_ref=src, dst_ref=dst, send_sem=sent, recv_sem=received,
            device_id=partner[level], device_id_type=MESH,
        )

    def copy(level, item):
        return remote(
            cur.at[level, item], got.at[level, item],
            send_sem.at[level, item], recv_sem.at[level, item], level,
        )

    def copy_raw(n):
        group = nd + (1 - side) * nf + n // 2
        src = w_hbm.at[pl.ds((n % 2) * half, half), group]
        return remote(src, raw.at[n], raw_send.at[n], raw_recv.at[n], top)

    copy_coord = remote(coord_hbm, coord_ref.at[1], coord_send, coord_recv, top)

    def copy_done(n, owner):
        dst = out_ref.at[pl.ds((n % 2) * half, half), nd + owner * nf + n // 2]
        return remote(done.at[n], dst, done_send.at[n], done_recv.at[n], top)

    copy_coord.start()
    for n in range(owned):
        copy_raw(n).start()

    spread = shuffle_matrix(half * 32, False)
    gather = shuffle_matrix(half * 32, True)

    def load(item):
        if item < direct + owned:
            if item % 2 == 0:
                fetches[item // 2].wait()
            first = (item % 2) * half
            stored = w_ref[first : first + half, group_of(item)]
        else:
            n = item - direct - owned
            copy_raw(n).wait_recv()
            stored = raw[n]
        moved = dot(spread, stored.reshape(half * 32, 128)).reshape(half, 2, 2 * SUB, 128)
        block = jnp.concatenate([moved[:, 0], moved[:, 1]], axis=-1)
        cur[0, item] = block.reshape(rows, rank).astype(BF16)
        copy(0, item).start()

    def place(which):
        if which == 0:
            fetch_coord.wait()
            fetch_slow.wait()
            padded[...] = jnp.zeros_like(padded)
        else:
            copy_coord.wait_recv()
        padded[0:2] = coord_ref[which].astype(F32)
        columns[which] = padded[...].T.reshape(columns.shape[1:])

    def angles(item, table, cos_ref, sin_ref):
        first = (item % 2) * half
        which = 1 if item >= direct + owned else 0
        column = columns[which, first : first + half, group_of(item)].reshape(half * SUB, 8)
        angle = column[:, 0:1] * slow_ref[table, 0:1] + column[:, 1:2] * slow_ref[table, 1:2]
        cosine, sine = cos_sin(angle)
        cos_ref[item] = cosine.reshape(half, SUB, rank)
        sin_ref[item] = sine.reshape(half, SUB, rank)

    def device_step(level, item):
        up = upper[level]
        mine = dot(cur[level, item], interp_ref[up, up])
        copy(level, item).wait_recv()
        summed = mine + dot(got[level, item], interp_ref[up, 1 - up])
        turned = rotate(summed.reshape(half, 2, SUB, rank), dcos[item], dsin[item])
        cur[level + 1, item] = turned.reshape(rows, rank).astype(BF16)
        if level + 1 < top or (level + 1 == top and item < direct):
            copy(level + 1, item).start()

    def local_steps(block, item):
        cosine = lcos[item : item + 2].reshape(high, SUB, rank)
        sine = lsin[item : item + 2].reshape(high, SUB, rank)
        for num in range(LOCAL):
            outer, inner = 1 << num, high >> (num + 1)
            pair = block.reshape(outer, 2, inner, 2 * SUB, rank)
            first = pair[:, 0].reshape(-1, rank)
            second = pair[:, 1].reshape(-1, rank)
            cos_pair = cosine.reshape(outer, 2, inner, SUB, rank)
            sin_pair = sine.reshape(outer, 2, inner, SUB, rank)
            results = []
            for target in range(2):
                summed = dot(first, interp_ref[target, 0]) + dot(second, interp_ref[target, 1])
                turned = rotate(
                    summed.reshape(outer * inner, 2, SUB, rank),
                    cos_pair[:, target].reshape(-1, SUB, rank),
                    sin_pair[:, target].reshape(-1, SUB, rank),
                )
                results.append(turned.astype(BF16).reshape(outer, inner, 2 * SUB, rank))
            block = jnp.stack(results, axis=1).reshape(high, 2 * SUB, rank)
        return block

    def as_stored(block, part):
        piece = block[part * half : (part + 1) * half]
        worked = jnp.stack([piece[..., :128], piece[..., 128:]], axis=1)
        stored = dot(gather, worked.reshape(half * 32, 128))
        return stored.reshape(half, 32, 128).astype(BF16)

    def finish(block, item):
        block = local_steps(block, item)
        for part in range(2):
            out_ref[part * half : (part + 1) * half, group_of(item)] = as_stored(block, part)

    def direct_end(k):
        block = cur[depth, 2 * k : 2 * k + 2].reshape(high, 2 * SUB, rank)
        finish(block, 2 * k)

    def owned_end(n, theirs):
        mine, other = direct + 2 * n, direct + owned + 2 * n
        target = 1 - side if theirs else side
        item = other if theirs else mine
        summed = dot(cur[top, mine : mine + 2].reshape(-1, rank), interp_ref[target, side])
        summed += dot(cur[top, other : other + 2].reshape(-1, rank), interp_ref[target, 1 - side])
        turned = rotate(
            summed.reshape(high, 2, SUB, rank),
            dcos[item : item + 2].reshape(high, SUB, rank),
            dsin[item : item + 2].reshape(high, SUB, rank),
        )
        block = turned.reshape(high, 2 * SUB, rank).astype(BF16)
        if not theirs:
            finish(block, item)
            return
        block = local_steps(block, item)
        for part in range(2):
            done[2 * n + part] = as_stored(block, part)
            copy_done(2 * n + part, side).start()

    tasks = []

    def task(when, work, *operands):
        tasks.append((when, len(tasks), work, operands))

    for item in range(items):
        theirs = item >= direct + owned
        begin = 3.8 + 2.8 * (item - direct - owned) if theirs else 0.1 * item
        task(begin, load, item)
        begin = begin + 0.8 if theirs else 1.0 + 0.3 * item
        task(begin, angles, item, 0, dcos, dsin)
        task(begin, device_step, 0, item)
        task(2.6 + 0.2 * item if item < direct else 3.0 + 1.4 * item, angles, item, 1, lcos, lsin)
        for level in range(1, top):
            when = 2.0 + 2.4 * level + 1.4 * item
            task(max(when, begin - 1.0 + 2.4 * level), device_step, level, item)
        if item < direct:
            task(2.6 + 2.4 * top + 2.8 * item, device_step, top, item)
    task(0.9, place, 0)
    task(0.95, fetch_interp.wait)
    task(3.5, place, 1)
    for k in range(nd):
        task(2.7 + 2.4 * top + 2.8 * (2 * k + 1), direct_end, k)
    for n in range(nf):
        last = direct + owned + 2 * n + 1
        when = 2.1 + 2.4 * (top - 1) + 1.4 * last
        when = max(when, 3.7 + 2.8 * (2 * n + 1) + 2.4 * (top - 1))
        task(when, owned_end, n, True)
        task(when + 3.0, owned_end, n, False)
    for _, _, work, operands in sorted(tasks, key=lambda entry: entry[:2]):
        work(*operands)

    for n in range(owned):
        copy_done(n, 1 - side).wait_recv()
        copy_raw(n).wait_send()
        copy_done(n, side).wait_send()
    copy_coord.wait_send()
    for level in range(depth):
        for item in range(items if level < top else direct):
            copy(level, item).wait_send()


def solution(mesh):
    levels = []
    for axis in ("bz", "by", "bx"):
        levels += [(axis, bit) for bit in range(mesh.shape[axis].bit_length() - 1)]

    def local(weights, interp, slowness, box_coord):
        per_dev, _, rank = weights.shape
        high = 1 << LOCAL
        nk = per_dev // (high * SUB)
        half = high // 2
        depth, chunks, rows = len(levels), 2 * nk, half * 2 * SUB
        stored = weights.reshape(per_dev, 2, 2, 128).transpose(0, 2, 1, 3)
        stored = stored.reshape(high, nk, 4 * SUB, 128)
        table = pltpu.VMEM((chunks, half, SUB, rank), F32)
        owned = nk // 4 * 2
        dma = pltpu.SemaphoreType.DMA
        result = pl.pallas_call(
            functools.partial(kernel, levels),
            out_shape=jax.ShapeDtypeStruct(stored.shape, BF16),
            in_specs=[pl.BlockSpec(memory_space=pltpu.HBM)] * 4,
            out_specs=pl.BlockSpec(memory_space=pltpu.VMEM),
            scratch_shapes=[
                pltpu.VMEM(stored.shape, BF16),
                pltpu.VMEM(interp.shape, BF16),
                pltpu.VMEM(slowness.shape, F32),
                pltpu.VMEM((2,) + box_coord.shape, jnp.int32),
                pltpu.VMEM((owned, half, 4 * SUB, 128), BF16),
                pltpu.VMEM((owned, half, 4 * SUB, 128), BF16),
                pltpu.VMEM((depth + 1, chunks, rows, rank), BF16),
                pltpu.VMEM((depth, chunks, rows, rank), BF16),
                table, table, table, table,
                pltpu.VMEM((8, per_dev), F32),
                pltpu.VMEM((2, high, nk, SUB, 8), F32),
                dma((nk + 3,)),
                dma((depth, chunks)), dma((depth, chunks)),
                dma((owned,)), dma((owned,)),
                dma, dma,
                dma((owned,)), dma((owned,)),
            ],
            compiler_params=pltpu.CompilerParams(
                collective_id=0, has_side_effects=True, vmem_limit_bytes=53 * 1024 * 1024
            ),
        )(stored, interp, slowness, box_coord)
        result = result.reshape(per_dev, 2, 2, 128).transpose(0, 2, 1, 3)
        return result.reshape(per_dev, 2, rank)

    return jax.shard_map(
        local,
        mesh=mesh,
        in_specs=(P(("shots", "bx", "by", "bz"), None, None), P(), P(), P(None, ("bx", "by", "bz"))),
        out_specs=P(("shots", "bx", "by", "bz"), None, None),
        check_vma=False,
    )
```

time: 44.1 us -> 42.2 us (0.957)
  local copies, waits for them, and re-layouts: 4.25 us -> 2.17 us
    unnamed x9 -> x5, local copies, waits for them, and re-layouts: 4.25 us -> 2.17 us
where the time goes in v2:
time: 42.2 us; the launch traced here: 42.1 us
  Pallas kernels  39.9 us (95%)
  local copies, waits for them, and re-layouts  2.17 us (5%)
    pallas_call x1, Pallas kernels, local(): pl.pallas_call(functools.partial(kernel, levels), out_shape=jax.ShapeDtyp...  39.9 us
    unnamed x5, local copies, waits for them, and re-layouts  2.17 us

profile of v2, /device:TPU:0, one launch (start us, length us, event | category | flops | bytes accessed | tf_op | source)
XLA Modules:
  0.0 42.1 jit_solution(13105292043506055358)
XLA Ops:
  0.0 0.0 copy-start
  0.0 0.7 %copy-done = f32[2,2,256]{2,1,0:T(2,128)S(1)} copy-done((f32[2,2,256]{2,1,0:T(2,128)S(1)}, f32[2,2,256]{2,1,0:T(2,128)}, u32[]{:S(2)}) %copy-start) | copy-done | bytes 4120
  0.7 0.0 copy-start.1
  0.7 0.7 %copy-done.1 = s32[2,512]{1,0:T(2,128)S(1)} copy-done((s32[2,512]{1,0:T(2,128)S(1)}, s32[2,512]{1,0:T(2,128)}, u32[]{:S(2)}) %copy-start.1) | copy-done | bytes 4120
  1.4 39.9 %shard_map.46 = bf16[16,4,32,128]{3,2,1,0:T(8,128)(2,1)S(1)} custom-call(bf16[16,4,32,128]{3,2,1,0:T(8,128)(2,1)} %bitcast.11, bf16[2,2,256,256]{3,2,1,0:T(8,128)(2,1)} %interp_hbm.1, f32[2,2,256]{2,1,0:T(2,128)S(1)} %copy-done, s32[2,512]{1,0:T(2,128)S(1)} %copy-done.1), custom_call_target="tpu_custom_call" | custom-call | tf_op jit(solution)/shard_map/pallas_call | solution.py:295
  41.3 0.8 %copy.8 = bf16[512,2,256]{2,1,0:T(2,128)(2,1)} copy(bf16[512,2,256]{2,1,0:T(2,128)(2,1)S(1)} %bitcast.10) | data formatting | bytes 1048576
Async XLA Ops:
  0.0 0.7 %copy-start = (f32[2,2,256]{2,1,0:T(2,128)S(1)}, f32[2,2,256]{2,1,0:T(2,128)}, u32[]{:S(2)}) copy-start(f32[2,2,256]{2,1,0:T(2,128)} %slow_hbm.1) | copy-start | bytes 12292
  0.7 0.7 %copy-start.1 = (s32[2,512]{1,0:T(2,128)S(1)}, s32[2,512]{1,0:T(2,128)}, u32[]{:S(2)}) copy-start(s32[2,512]{1,0:T(2,128)} %coord_hbm.1) | copy-start | bytes 12292

commit v3 on v2

--- a/solution.py
+++ b/solution.py
@@ -127,8 +127,6 @@
         return remote(done.at[n], dst, done_send.at[n], done_recv.at[n], top)
 
     copy_coord.start()
-    for n in range(owned):
-        copy_raw(n).start()
 
     spread = shuffle_matrix(half * 32, False)
     gather = shuffle_matrix(half * 32, True)
@@ -234,6 +232,9 @@
             done[2 * n + part] = as_stored(block, part)
             copy_done(2 * n + part, side).start()
 
+    def start_raw(n):
+        copy_raw(n).start()
+
     tasks = []
 
     def task(when, work, *operands):
@@ -241,7 +242,7 @@
 
     for item in range(items):
         theirs = item >= direct + owned
-        begin = 3.8 + 2.8 * (item - direct - owned) if theirs else 0.1 * item
+        begin = 6.0 + 2.8 * (item - direct - owned) if theirs else 0.1 * item
         task(begin, load, item)
         begin = begin + 0.8 if theirs else 1.0 + 0.3 * item
         task(begin, angles, item, 0, dcos, dsin)
@@ -252,6 +253,8 @@
             task(max(when, begin - 1.0 + 2.4 * level), device_step, level, item)
         if item < direct:
             task(2.6 + 2.4 * top + 2.8 * item, device_step, top, item)
+    for n in range(owned):
+        task((-1.0, 5.0)[n % 2], start_raw, n)
     task(0.9, place, 0)
     task(0.95, fetch_interp.wait)
     task(3.5, place, 1)

time: 42.2 us -> 41.8 us (level)
  Pallas kernels: 39.9 us -> 39.4 us
    pallas_call x1, Pallas kernels: 39.9 us -> 39.4 us  [local(): pl.pallas_call(functools.partial(kernel, levels), out_shape=jax.ShapeDtyp...]
where the time goes in v3:
time: 41.8 us; the launch traced here: 41.6 us
  Pallas kernels  39.4 us (94%)
  local copies, waits for them, and re-layouts  2.17 us (5%)
    pallas_call x1, Pallas kernels, local(): pl.pallas_call(functools.partial(kernel, levels), out_shape=jax.ShapeDtyp...  39.4 us
    unnamed x5, local copies, waits for them, and re-layouts  2.17 us

profile of v3, /device:TPU:0, one launch (start us, length us, event | category | flops | bytes accessed | tf_op | source)
XLA Modules:
  0.0 41.6 jit_solution(16026785487525481601)
XLA Ops:
  0.0 0.0 copy-start
  0.0 0.7 %copy-done = f32[2,2,256]{2,1,0:T(2,128)S(1)} copy-done((f32[2,2,256]{2,1,0:T(2,128)S(1)}, f32[2,2,256]{2,1,0:T(2,128)}, u32[]{:S(2)}) %copy-start) | copy-done | bytes 4120
  0.7 0.0 copy-start.1
  0.7 0.7 %copy-done.1 = s32[2,512]{1,0:T(2,128)S(1)} copy-done((s32[2,512]{1,0:T(2,128)S(1)}, s32[2,512]{1,0:T(2,128)}, u32[]{:S(2)}) %copy-start.1) | copy-done | bytes 4120
  1.4 39.4 %shard_map.46 = bf16[16,4,32,128]{3,2,1,0:T(8,128)(2,1)S(1)} custom-call(bf16[16,4,32,128]{3,2,1,0:T(8,128)(2,1)} %bitcast.11, bf16[2,2,256,256]{3,2,1,0:T(8,128)(2,1)} %interp_hbm.1, f32[2,2,256]{2,1,0:T(2,128)S(1)} %copy-done, s32[2,512]{1,0:T(2,128)S(1)} %copy-done.1), custom_call_target="tpu_custom_call" | custom-call | tf_op jit(solution)/shard_map/pallas_call | solution.py:298
  40.8 0.8 %copy.8 = bf16[512,2,256]{2,1,0:T(2,128)(2,1)} copy(bf16[512,2,256]{2,1,0:T(2,128)(2,1)S(1)} %bitcast.10) | data formatting | bytes 1048576
Async XLA Ops:
  0.0 0.7 %copy-start = (f32[2,2,256]{2,1,0:T(2,128)S(1)}, f32[2,2,256]{2,1,0:T(2,128)}, u32[]{:S(2)}) copy-start(f32[2,2,256]{2,1,0:T(2,128)} %slow_hbm.1) | copy-start | bytes 12292
  0.7 0.7 %copy-start.1 = (s32[2,512]{1,0:T(2,128)S(1)}, s32[2,512]{1,0:T(2,128)}, u32[]{:S(2)}) copy-start(s32[2,512]{1,0:T(2,128)} %coord_hbm.1) | copy-start | bytes 12292
